TPU v7x, 128 devices: a whole 4x4x4 slice. The times are simulated.
128 devices in a mesh: leaf: 32 (over z_hi, y, x), blk: 4 (over z_lo, core).
Axes of the slice: x: 4, y: 4, z: 4 (z_hi: 2, z_lo: 2; z = z_hi * 2 + z_lo), core: 2. Of those that a mesh axis runs over, the one named last changes fastest.
Arguments:
- schur: bfloat16 [32, 3, 2048, 2048], P('leaf', None, 'blk'), as said below
- modes: bfloat16 [32, 3, 2048, 512], P('leaf', None, 'blk'), may hold values from -0.125 to 0.125
- counts: int32 [32, 3], P('leaf'), may hold values from 128 to 512, as said below
Outputs:
- reduced: float32 [32, 3, 512, 512], P('leaf', None, 'blk')
Inputs may be any that keep to these rules, and one draw needn't show every extreme that they name: `counts`: each entry lies from 128 to 512; some subtree keeps exactly 512. Each block schur[i, k] is symmetric with a dominant positive diagonal.
All inputs are finite; a program needn't handle non-finite values.
Results may differ from a plain program's by a relative error of at most 0.0016.
Values may be sent and summed in bfloat16 or wider, within the bound.
A program may use at most 128 MiB of HBM per device.

v0:
```python
import jax
import jax.numpy as jnp
from jax import lax
from jax.sharding import PartitionSpec as P

LEV = 2


def swapped(shard, axis, stride):
    return lax.ppermute(shard, axis, [(i, i ^ 1 << stride) for i in range(lax.axis_size(axis))])


def add_rows(block, piece):
    return jnp.einsum("ksr,krc->ksc", block, piece, preferred_element_type=jnp.float32)


def shards(schur, modes, counts):
    summed = schur.astype(jnp.float32)
    first_level = 0
    for level in range(first_level, LEV):
        summed = summed + swapped(summed, "leaf", level)
    merged = summed.astype(jnp.bfloat16)
    column = jnp.arange(modes.shape[-1], dtype=jnp.int32)
    keep = column[None, None, None, :] < counts[:, :, None, None]
    kept = jnp.where(keep, modes, jnp.zeros_like(modes))
    local_rows = merged[0]
    local_kept = kept[0]
    pieces = []
    for slot in range(local_rows.shape[0]):
        single_rows = local_rows[slot : slot + 1]
        empty_one = jnp.zeros((1, local_rows.shape[1], local_kept.shape[2]), jnp.float32)

        def add_one(total, piece, start, single_rows=single_rows):
            return add_rows(single_rows, piece)

        pieces.append(
            add_one(
                empty_one,
                lax.all_gather(local_kept[slot : slot + 1], "blk", axis=1, tiled=True),
                jnp.int32(0),
            )
        )
    projected = jnp.concatenate(pieces, axis=0)
    projected = projected.astype(jnp.bfloat16)
    terms = jnp.einsum("krc,krd->kcd", local_kept, projected, preferred_element_type=jnp.float32)
    reduced = lax.psum_scatter(terms, "blk", scatter_dimension=1, tiled=True)
    return reduced[None]


def solution(mesh):
    placed = (P("leaf", None, "blk", None), P("leaf", None, "blk", None), P("leaf", None))
    return jax.shard_map(
        shards, mesh=mesh, in_specs=placed, out_specs=P("leaf", None, "blk", None), check_vma=False
    )
```

profile of v0, /device:TPU:1, one launch (start us, length us, event | category | flops | bytes accessed | tf_op | source)
XLA Modules:
  0.0 642.3 jit_solution(13706043693440139582)
XLA Ops:
  6.5 0.0 all-gather.7.cloned.1.call-start
  6.5 4.2 convert_element_type.7
  10.8 0.0 copy-start.1
  10.8 0.0 copy-start
  10.8 2.1 collective-permute-start
  12.9 269.7 %collective-permute-done = f32[1,3,512,2048]{3,2,1,0:T(8,128)} collective-permute-done((f32[1,3,512,2048]{3,2,1,0:T(8,128)S(1)}, f32[1,3,512,2048]{3,2,1,0:T(8,128)}, u32[]{:S(2)}, u32[]{:S(2)}) %collective-permute-start) | collective-permute-done | bytes 12582944 | tf_op jit(solution)/shard_map/ppermute | solution.py:10
  282.6 14.2 %convert_add_fusion = f32[1,3,512,2048]{3,2,1,0:T(8,128)} fusion(f32[1,3,512,2048]{3,2,1,0:T(8,128)} %collective-permute-done, bf16[1,3,512,2048]{3,2,1,0:T(8,128)(2,1)} %param.3), kind=kLoop, calls=%fused_computation.1 | loop fusion | flops 6291456 | bytes 31457280 | tf_op jit(solution)/shard_map/add | solution.py:21
  296.8 3.2 collective-permute-start.1
  300.0 0.0 copy-done.1
  300.0 0.1 iota_compare_fusion
  300.0 0.0 copy-done
  300.0 0.1 broadcast_select_fusion
  300.1 1.2 fusion.32
  301.4 0.0 all-gather.7.cloned.1.call-update
  301.4 0.0 all-gather.9.cloned.1.call-start
  301.4 0.7 all-gather.9.cloned.1.call-update
  302.1 0.0 all-gather.11.cloned.1.call-start
  302.2 0.7 all-gather.11.cloned.1.call-update
  302.9 0.0 reduce-scatter.2.cloned.1.call-start
  302.9 266.2 %collective-permute-done.1 = f32[1,3,512,2048]{3,2,1,0:T(8,128)} collective-permute-done((f32[1,3,512,2048]{3,2,1,0:T(8,128)}, f32[1,3,512,2048]{3,2,1,0:T(8,128)}, u32[]{:S(2)}, u32[]{:S(2)}) %collective-permute-start.1) | collective-permute-done | bytes 12582944 | tf_op jit(solution)/shard_map/ppermute | solution.py:10
  569.1 11.8 %add_convert_fusion = bf16[1,3,512,2048]{3,2,1,0:T(8,128)(2,1)} fusion(f32[1,3,512,2048]{3,2,1,0:T(8,128)} %convert_add_fusion, f32[1,3,512,2048]{3,2,1,0:T(8,128)} %collective-permute-done.1), kind=kLoop, calls=%fused_computation | loop fusion | flops 6291456 | bytes 31457280 | tf_op jit(solution)/shard_map/convert_element_type | solution.py:22
  580.9 0.0 all-gather.7.cloned.1.call-done
  580.9 3.5 fusion.28
  584.4 0.0 all-gather.9.cloned.1.call-done
  584.4 3.5 fusion.25
  587.9 0.0 all-gather.11.cloned.1.call-done
  587.9 3.5 fusion.22
  591.4 2.7 fusion.6
  594.1 0.0 reduce-scatter.2.cloned.1.call-update
  594.1 41.6 %reduce-scatter.2.cloned.1.call-done = f32[3,128,512]{2,1,0:T(8,128)} async-done(((f32[3,512,512]{2,1,0:T(8,128)}), f32[3,128,512]{2,1,0:T(8,128)}) %reduce-scatter.2.cloned.1.call-update) | async-done | bytes 786448 | tf_op jit(solution)/shard_map/reduce_scatter | solution.py:46
Async XLA Ops:
  6.5 574.4 %all-gather.7.cloned.1.call-start = ((), (), s32[]{:S(2)}) async-start(), calls=%async_computation.2 | async-start | bytes 2621440 | tf_op jit(solution)/shard_map/all_gather | solution.py:39
  10.8 289.2 %copy-start.1 = (s32[1,3]{1,0:T(1,128)S(1)}, s32[1,3]{1,0:T(1,128)}, u32[]{:S(2)}) copy-start(s32[1,3]{1,0:T(1,128)} %param.5) | copy-start | bytes 40
  10.8 289.2 %copy-start = (bf16[1,3,512,512]{3,2,1,0:T(8,128)(2,1)S(1)}, bf16[1,3,512,512]{3,2,1,0:T(8,128)(2,1)}, u32[]{:S(2)}) copy-start(bf16[1,3,512,512]{3,2,1,0:T(8,128)(2,1)} %param.4) | copy-start | bytes 4718596
  10.8 271.8 %collective-permute-start = (f32[1,3,512,2048]{3,2,1,0:T(8,128)S(1)}, f32[1,3,512,2048]{3,2,1,0:T(8,128)}, u32[]{:S(2)}, u32[]{:S(2)}) collective-permute-start(f32[1,3,512,2048]{3,2,1,0:T(8,128)S(1)} %convert_element_type.7), channel_id=1, source_target_pairs={{0,4},{4,0},{8,12},{12,8},{16,20},{20,16},{24,28},{28,24},{32,36},... | collective-permute-start | bytes 37748744 | tf_op jit(solution)/shard_map/ppermute | solution.py:10
  296.8 272.3 %collective-permute-start.1 = (f32[1,3,512,2048]{3,2,1,0:T(8,128)}, f32[1,3,512,2048]{3,2,1,0:T(8,128)}, u32[]{:S(2)}, u32[]{:S(2)}) collective-permute-start(f32[1,3,512,2048]{3,2,1,0:T(8,128)} %convert_add_fusion), channel_id=1, source_target_pairs={{0,8},{4,12},{8,0},{12,4},{16,24},{20,28},{24,16},{28,20},{32,40},... | collective-permute-start | bytes 37748744 | tf_op jit(solution)/shard_map/ppermute | solution.py:10
  301.4 283.1 %all-gather.9.cloned.1.call-start = ((), (), s32[]{:S(2)}) async-start(), calls=%async_computation.3 | async-start | bytes 2621440 | tf_op jit(solution)/shard_map/all_gather | solution.py:39
  302.1 285.8 %all-gather.11.cloned.1.call-start = ((), (), s32[]{:S(2)}) async-start(), calls=%async_computation.4 | async-start | bytes 2621440 | tf_op jit(solution)/shard_map/all_gather | solution.py:39
  302.9 332.9 %reduce-scatter.2.cloned.1.call-start = ((), (), s32[]{:S(2)}) async-start(), calls=%async_computation.1 | async-start | bytes 3932160 | tf_op jit(solution)/shard_map/reduce_scatter | solution.py:46
Sparse Core Ops, SparseCore 0:
  301.5 31.5 all-gather.6
  334.7 30.3 all-gather.8
  366.8 30.3 all-gather.10
  594.2 41.4 reduce-scatter.1
where the time goes:
time: 642 us
  waiting for transfers between devices  579 us (90%)
  other arithmetic  30.4 us (5%)
  between operations  13.2 us (2%)
  matrix products  13.1 us (2%)
    ppermute x2, waiting for transfers between devices, swapped(): lax.ppermute(shard, axis, [(i, i ^ 1 << stride) for i in range(lax.axis_s...  536 us
    reduce_scatter x1, waiting for transfers between devices, shards(): reduced = lax.psum_scatter(terms, 'blk', scatter_dimension=1, tiled=True)  41.6 us
    add x1, other arithmetic, shards(): summed = summed + swapped(summed, 'leaf', level)  14.2 us
  transfers between devices with their start and end apart: 6, of which 3 were waited for; matrix products, arithmetic and copies ran while one was open for 3% of the time, Pallas kernels for 0%

commit v1 on v0

v1 whole, which is shorter than its diff:
```python
import functools

import jax
import jax.numpy as jnp
from jax import lax
from jax.experimental import pallas as pl
from jax.experimental.pallas import tpu as pltpu
from jax.sharding import PartitionSpec as P

MESH = pl.DeviceIdType.MESH
ANY = pl.BlockSpec(memory_space=pl.ANY)
F32 = jnp.float32
BF16 = jnp.bfloat16

SUB = 3
N = 512
Q = 128
RING = 4


def dot(a, b):
    return jnp.dot(a, b, preferred_element_type=F32)


def dot_rows(a, b):
    return lax.dot_general(a, b, (((0,), (0,)), ((), ())), preferred_element_type=F32)


def kernel(
    schur, modes, out,
    raw, raw_a, m, m_a, vo, vn, vz, red, red_c, red_s, red_z,
    rs_s, rs_r, a_s, a_r, ga_s, ga_r, ag_s, ag_r, v_l, v_s, v_r, r_s, r_r, o_s,
):
    leaf = lax.axis_index("leaf")
    blk = lax.axis_index("blk")
    x = lax.rem(leaf, RING)
    base = leaf - x
    z, core = blk // 2, lax.rem(blk, 2)
    right = (base + lax.rem(x + 1, RING), blk)
    left = (base + lax.rem(x + RING - 1, RING), blk)
    across = (base + lax.rem(x + 2, RING), blk)
    twin = (leaf, z * 2 + 1 - core)
    other = (leaf, (1 - z) * 2 + core)

    nxt = lax.rem(blk + 1, 4) * N
    opp = lax.rem(blk + 2, 4) * N
    own = blk * N

    def remote(src, dst, send, recv, to):
        return pltpu.make_async_remote_copy(
            src_ref=src, dst_ref=dst, send_sem=send, recv_sem=recv, device_id=to, device_id_type=MESH
        )

    def arrived(ref, sem):
        pltpu.make_async_copy(ref, ref, sem).wait()

    for k in range(SUB):
        pltpu.make_async_copy(modes.at[0, k], vo.at[k], v_l.at[k]).start()

    barrier = pltpu.get_barrier_semaphore()
    for device in (right, left, across, twin, other):
        pl.semaphore_signal(barrier, inc=1, device_id=device, device_id_type=MESH)
    pl.semaphore_wait(barrier, 5)

    def parts(k, d):
        rows = pl.ds(d * Q, Q)
        yield schur.at[0, k, rows, pl.ds(pl.multiple_of(nxt, Q), N)], (k, 0, slice(None), slice(None))
        yield (
            schur.at[0, k, rows, pl.ds(pl.multiple_of(own + d * Q, Q), N - d * Q)],
            (k, 1, slice(None), pl.ds(d * Q, N - d * Q)),
        )
        if d:
            yield (
                schur.at[0, k, rows, pl.ds(pl.multiple_of(opp, Q), d * Q)],
                (k, 1, slice(None), pl.ds(0, d * Q)),
            )

    def scatter(k):
        for d in range(RING):

            @pl.when(x == d)
            def _():
                for src, at in parts(k, d):
                    pltpu.make_async_copy(src, raw.at[(x, *at)], rs_r.at[x, k]).start()

            @pl.when(x != d)
            def _():
                for src, at in parts(k, d):
                    remote(src, raw.at[(x, *at)], rs_s.at[d, k], rs_r.at[x, k], (base + d, blk)).start()

    def scatter_a():
        for d in range(RING):
            at = z * 256 + (d // 2) * Q
            src = schur.at[
                0, :, pl.ds(pl.multiple_of(at + (d % 2) * 64, 64), 64), pl.ds(pl.multiple_of(opp + at, Q), Q)
            ]

            @pl.when(x == d)
            def _():
                pltpu.make_async_copy(src, raw_a.at[x], a_r.at[x]).start()

            @pl.when(x != d)
            def _():
                remote(src, raw_a.at[x], a_s.at[d], a_r.at[x], (base + d, blk)).start()

    def total(ref, *at):
        t = [ref[(j, *at)].astype(F32) for j in range(RING)]
        return (t[0] + t[1]) + (t[2] + t[3])

    mine = pl.ds(pl.multiple_of(x * Q, Q), Q)
    from_left = pl.ds(pl.multiple_of(lax.rem(x + RING - 1, RING) * Q, Q), Q)
    from_right = pl.ds(pl.multiple_of(lax.rem(x + 1, RING) * Q, Q), Q)
    from_across = pl.ds(pl.multiple_of(lax.rem(x + 2, RING) * Q, Q), Q)

    def merge(k):
        for j in range(RING):
            arrived(raw.at[j, k], rs_r.at[j, k])
        m[k, 0, mine, :] = total(raw, k, 0).astype(BF16)
        column = lax.broadcasted_iota(jnp.int32, (Q, N), 1) // Q
        weight = jnp.where(column == x, 0.5, 1.0)
        m[k, 1, mine, :] = (total(raw, k, 1) * weight).astype(BF16)

    def gather(k):
        return [
            remote(m.at[k, t, mine], m.at[k, t, mine], ag_s.at[k, side, t], ag_r.at[k, side, t], to)
            for t, side, to in ((0, 0, right), (1, 1, left), (1, 0, right), (0, 1, left))
        ]

    def relay(k):
        return [
            remote(m.at[k, 0, from_left], m.at[k, 0, from_left], ag_s.at[k, 0, 2], ag_r.at[k, 0, 2], right),
            remote(m.at[k, 1, from_right], m.at[k, 1, from_right], ag_s.at[k, 1, 2], ag_r.at[k, 1, 2], left),
        ]

    def start_relay(k):
        arrived(m.at[k, 0, from_left], ag_r.at[k, 0, 0])
        relay(k)[0].start()
        arrived(m.at[k, 1, from_right], ag_r.at[k, 1, 1])
        relay(k)[1].start()

    def gathered(k):
        arrived(m.at[k, 1, from_left], ag_r.at[k, 0, 1])
        arrived(m.at[k, 0, from_right], ag_r.at[k, 1, 0])
        arrived(m.at[k, 0, from_across], ag_r.at[k, 0, 2])
        arrived(m.at[k, 1, from_across], ag_r.at[k, 1, 2])

    def gather_a():
        return [
            remote(m_a.at[x], m_a.at[x], ga_s.at[i], ga_r.at[x], to) for i, to in enumerate((right, left, across))
        ]

    def to_other(k):
        return remote(modes.at[0, k], vz.at[k], v_s.at[k, 0], v_r.at[k, 0], other)

    def to_twin(k, src):
        return remote(src, vn.at[k], v_s.at[k, 1], v_r.at[k, 1], twin)

    def pass_modes(k):
        arrived(vz.at[k], v_r.at[k, 0])

        @pl.when(core == 0)
        def _():
            to_twin(k, vz.at[k]).start()

    def project(k):
        gathered(k)
        arrived(vo.at[k], v_l.at[k])
        arrived(vn.at[k], v_r.at[k, 1])
        row = lax.broadcasted_iota(jnp.int32, (N, N), 0) // Q
        column = lax.broadcasted_iota(jnp.int32, (N, N), 1) // Q
        quarter = m[k, 1]
        zero = jnp.zeros_like(quarter)
        p = dot(m[k, 0], vn[k])
        p += dot(jnp.where(column >= row, quarter, zero), vo[k])
        lone = jnp.concatenate([m_a[d, k] for d in range(RING)], axis=0)
        lone = jnp.concatenate([lone, lone], axis=0)
        lone = jnp.concatenate([lone] * 4, axis=1)
        diagonal = (column == row) & (row // 2 == z)
        p += dot(jnp.where(column < row, quarter, jnp.where(diagonal, lone, zero)), vz[k])
        p = p.astype(BF16)
        red[k] = dot_rows(vo[k], p) + dot_rows(p, vo[k])

    def slab(i, c):
        return pl.ds(pl.multiple_of((2 * i + c) * Q, Q), Q)

    def swap_cores(k):
        return [
            remote(red.at[k, slab(i, 1 - core)], red_c.at[k, i], r_s.at[k, i], r_r.at[k, i], twin) for i in range(2)
        ]

    def swap_chips(k):
        return remote(red_s.at[k], red_z.at[k], r_s.at[k, 2], r_r.at[k, 2], other)

    def add_cores(k):
        for i in range(2):
            arrived(red_c.at[k, i], r_r.at[k, i])
        red_s[k] = red[k, slab(1 - z, core), :] + red_c[k, 1 - z]
        swap_chips(k).start()
        red_c[k, z] = red[k, slab(z, core), :] + red_c[k, z]

    def finish(k):
        arrived(red_z.at[k], r_r.at[k, 2])
        red_c[k, z] = red_c[k, z] + red_z[k]
        return pltpu.make_async_copy(red_c.at[k, z], out.at[k], o_s.at[k])

    def start(copies):
        for c in copies:
            c.start()

    scatter(0)
    for k in range(SUB):
        to_other(k).start()

    @pl.when(core == 1)
    def _():
        for k in range(SUB):
            to_twin(k, modes.at[0, k]).start()

    scatter_a()
    scatter(1)
    merge(0)
    start(gather(0))
    scatter(2)
    for j in range(RING):
        arrived(raw_a.at[j], a_r.at[j])
    m_a[x] = total(raw_a).astype(BF16)
    start(gather_a())
    pass_modes(0)
    merge(1)
    start(gather(1))
    start_relay(0)
    pass_modes(1)
    for d in range(1, RING):
        arrived(m_a.at[lax.rem(x + d, RING)], ga_r.at[lax.rem(x + d, RING)])
    project(0)
    start(swap_cores(0))
    merge(2)
    start(gather(2))
    add_cores(0)
    start_relay(1)
    pass_modes(2)
    project(1)
    start(swap_cores(1))
    start_relay(2)
    add_cores(1)
    finish(0).start()
    project(2)
    start(swap_cores(2))
    finish(1).start()
    add_cores(2)
    finish(2).start()

    for k in range(SUB):
        for d in range(RING):

            @pl.when(x != d)
            def _():
                arrived(raw.at[0, k], rs_s.at[d, k])

        for c in gather(k) + relay(k) + [to_other(k), to_twin(k, vz.at[k]), *swap_cores(k), swap_chips(k)]:
            c.wait_send()
        pltpu.make_async_copy(red_c.at[k, z], out.at[k], o_s.at[k]).wait()
    for d in range(RING):

        @pl.when(x != d)
        def _():
            arrived(raw_a.at[0], a_s.at[d])

    for c in gather_a():
        c.wait_send()


def shards(schur, modes, counts):
    dma = pltpu.SemaphoreType.DMA
    reduced = pl.pallas_call(
        kernel,
        out_shape=jax.ShapeDtypeStruct((SUB, Q, N), F32),
        in_specs=[ANY, ANY],
        out_specs=ANY,
        scratch_shapes=[
            pltpu.VMEM((RING, SUB, 2, Q, N), BF16),
            pltpu.VMEM((RING, SUB, 64, Q), BF16),
            pltpu.VMEM((SUB, 2, N, N), BF16),
            pltpu.VMEM((RING, SUB, 64, Q), BF16),
            pltpu.VMEM((SUB, N, N), BF16),
            pltpu.VMEM((SUB, N, N), BF16),
            pltpu.VMEM((SUB, N, N), BF16),
            pltpu.VMEM((SUB, N, N), F32),
            pltpu.VMEM((SUB, 2, Q, N), F32),
            pltpu.VMEM((SUB, Q, N), F32),
            pltpu.VMEM((SUB, Q, N), F32),
            dma((RING, SUB)), dma((RING, SUB)),
            dma((RING,)), dma((RING,)),
            dma((3,)), dma((RING,)),
            dma((SUB, 2, 3)), dma((SUB, 2, 3)),
            dma((SUB,)), dma((SUB, 2)), dma((SUB, 2)),
            dma((SUB, 3)), dma((SUB, 3)),
            dma((SUB,)),
        ],
        compiler_params=pltpu.CompilerParams(
            collective_id=0, has_side_effects=True, vmem_limit_bytes=56 << 20
        ),
        cost_estimate=pl.CostEstimate(flops=5 * SUB * 2 * N**3, bytes_accessed=8 << 20, transcendentals=0),
        name="merge_and_project",
    )(schur, modes)
    row = lax.axis_index("blk") * Q + lax.broadcasted_iota(jnp.int32, reduced.shape, 1)
    column = lax.broadcasted_iota(jnp.int32, reduced.shape, 2)
    kept = counts[0][:, None, None]
    return jnp.where((row < kept) & (column < kept), reduced, 0.0)[None]


def solution(mesh):
    placed = (P("leaf", None, "blk", None), P("leaf", None, "blk", None), P("leaf", None))
    return jax.shard_map(
        shards, mesh=mesh, in_specs=placed, out_specs=P("leaf", None, "blk", None), check_vma=False
    )
```

time: 642 us -> 91.7 us (0.14)
  waiting for transfers between devices: 579 us -> 0 us
  Pallas kernels: 0 us -> 89.4 us
  other arithmetic: 30.4 us -> 2.15 us
  between operations: 13.2 us -> 0.02 us
  matrix products: 13.1 us -> 0 us
    ppermute x2 -> x0, waiting for transfers between devices: 536 us -> none  [swapped(): lax.ppermute(shard, axis, [(i, i ^ 1 << stride) for i in range(lax.axis_s...]
    pallas_call x0 -> x1, Pallas kernels: none -> 89.4 us  [shards(): pl.pallas_call(kernel, out_shape=jax.ShapeDtypeStruct((SUB, Q, N), F32),...]
    reduce_scatter x1 -> x0, waiting for transfers between devices: 41.6 us -> none  [shards(): reduced = lax.psum_scatter(terms, 'blk', scatter_dimension=1, tiled=True)]
    convert_element_type x2 -> x0, other arithmetic: 16.1 us -> none  [the longest x1 11.8 us: shards(): merged = summed.astype(jnp.bfloat16)]
    add x1, other arithmetic: 14.2 us -> 0.01 us  [shards(): lax.axis_index('blk') * Q]
    dot_general x4 -> x0, matrix products: 13.1 us -> none  [the longest x3 10.4 us: add_rows(): jnp.einsum('ksr,krc->ksc', block, piece, preferred_element_type=jnp.float32)]
  transfers between devices with their start and end apart: 6 -> 0, of which waited for: 3 -> 0; matrix products, arithmetic and copies ran while one was open for 3% -> 0% of each run, Pallas kernels for 0% -> 0%
where the time goes in v1:
time: 91.7 us; the launch traced here: 91.6 us
  Pallas kernels  89.4 us (97%)
  other arithmetic  2.15 us (2%)
    pallas_call x1, Pallas kernels, shards(): pl.pallas_call(kernel, out_shape=jax.ShapeDtypeStruct((SUB, Q, N), F32),...  89.4 us
    broadcast_in_dim x1, other arithmetic, shards(): return jnp.where((row < kept) & (column < kept), reduced, 0.0)[None]  2.15 us

profile of v1, /device:TPU:1, one launch (start us, length us, event | category | flops | bytes accessed | tf_op | source)
XLA Modules:
  0.0 91.6 jit_solution(4682038193055820699)
XLA Ops:
  0.0 0.0 copy-start
  0.0 89.4 %merge_and_project.1 = f32[3,128,512]{2,1,0:T(8,128)} custom-call(bf16[1,3,512,2048]{3,2,1,0:T(8,128)(2,1)} %schur.1, bf16[1,3,512,512]{3,2,1,0:T(8,128)(2,1)} %modes.1), custom_call_target="tpu_custom_call" | custom-call | flops 4026531840 | bytes 8388608 | tf_op jit(solution)/shard_map/merge_and_project/pallas_call | solution.py:275
  89.4 0.0 copy-done
  89.4 2.2 %select_bitcast_fusion = f32[1,3,128,512]{3,2,1,0:T(8,128)} fusion(f32[3,128,512]{2,1,0:T(8,128)} %merge_and_project.1, s32[3]{0:T(128)S(1)} %bitcast.3, s32[128]{0:T(128)S(1)} %iota_add_fusion), kind=kLoop, calls=%fused_computation | loop fusion | flops 786432 | bytes 1573388 | tf_op jit(solution)/shard_map/broadcast_in_dim | solution.py:309
  (1 shorter events, 0.0 us)
Async XLA Ops:
  0.0 89.4 %copy-start = (s32[1,3]{1,0:T(1,128)S(1)}, s32[1,3]{1,0:T(1,128)}, u32[]{:S(2)}) copy-start(s32[1,3]{1,0:T(1,128)} %param.5) | copy-start | bytes 40

commit v2 on v0

v2 whole, which is shorter than its diff:
```python
import jax
import jax.numpy as jnp
from jax import lax
from jax.experimental import pallas as pl
from jax.experimental.pallas import tpu as pltpu
from jax.sharding import PartitionSpec as P

MESH = pl.DeviceIdType.MESH
ANY = pl.BlockSpec(memory_space=pl.ANY)
F32 = jnp.float32
BF16 = jnp.bfloat16

SUB = 3
N = 512
Q = 128
RING = 4


def dot(a, b):
    return jnp.dot(a, b, preferred_element_type=F32)


def dot_rows(a, b):
    return lax.dot_general(a, b, (((0,), (0,)), ((), ())), preferred_element_type=F32)


def kernel(
    schur, modes, out,
    db, ob, qp, near, inbox, part, m, diag, dg, vo, vn, vz, red, red_c, red_s, red_z, last_s, last_z,
    ld, rs_s, rs_r, d_s, d_r, ag_s, ag_r, v_s, v_r, r_s, r_r, o_s,
):
    leaf = lax.axis_index("leaf")
    blk = lax.axis_index("blk")
    x = lax.rem(leaf, RING)
    base = leaf - x
    z, core = blk // 2, lax.rem(blk, 2)
    x1, x2, x3 = (lax.rem(x + i, RING) for i in (1, 2, 3))
    right, across, left = ((base + i, blk) for i in (x1, x2, x3))
    twin = (leaf, z * 2 + 1 - core)
    other = (leaf, (1 - z) * 2 + core)

    def columns(i):
        return pl.ds(pl.multiple_of(lax.rem(blk + i, 4) * N, N), N)

    def quarter(d):
        return pl.ds(pl.multiple_of(d * Q, Q), Q)

    def remote(src, dst, send, recv, to):
        return pltpu.make_async_remote_copy(
            src_ref=src, dst_ref=dst, send_sem=send, recv_sem=recv, device_id=to, device_id_type=MESH
        )

    def arrived(ref, sem):
        pltpu.make_async_copy(ref, ref, sem).wait()

    def start(*copies):
        for c in copies:
            c.start()

    def load(k):
        for i, (src, dst) in enumerate((
            (schur.at[0, k, :, columns(0)], db.at[k]),
            (schur.at[0, k, :, columns(2)], ob.at[k]),
            (schur.at[0, k, quarter(x1), columns(1)], near.at[k, 1]),
            (schur.at[0, k, quarter(x), columns(1)], near.at[k, 0]),
            (modes.at[0, k], vo.at[k]),
        )):
            pltpu.make_async_copy(src, dst, ld.at[k, i]).start()

    def raw(k):
        return (
            remote(schur.at[0, k, quarter(x2), columns(1)], inbox.at[k, 0], rs_s.at[k, 0], rs_r.at[k, 0], right),
            remote(schur.at[0, k, quarter(x3), columns(1)], inbox.at[k, 1], rs_s.at[k, 1], rs_r.at[k, 1], left),
            remote(qp.at[k, quarter(x2)], inbox.at[k, 3], rs_s.at[k, 3], rs_r.at[k, 3], left),
            remote(qp.at[k, quarter(x1)], inbox.at[k, 4], rs_s.at[k, 4], rs_r.at[k, 4], right),
        )

    def partial(k):
        return (
            remote(part.at[k, 0], inbox.at[k, 2], rs_s.at[k, 2], rs_r.at[k, 2], right),
            remote(part.at[k, 1], inbox.at[k, 5], rs_s.at[k, 5], rs_r.at[k, 5], left),
        )

    def come(k, i):
        arrived(inbox.at[k, i], rs_r.at[k, i])
        return inbox[k, i].astype(F32)

    ri = lax.broadcasted_iota(jnp.int32, (Q, Q), 0)
    ci = lax.broadcasted_iota(jnp.int32, (Q, Q), 1)

    def at(r):
        return slice(r * Q, (r + 1) * Q)

    def pack(k):
        arrived(db.at[k], ld.at[k, 0])
        arrived(ob.at[k], ld.at[k, 1])
        for r in range(4):
            if r:
                qp[k, at(r), : r * Q] = ob[k, at(r), : r * Q]
            if r < 3:
                qp[k, at(r), (r + 1) * Q :] = db[k, at(r), (r + 1) * Q :]
            if r % 2:
                a, b = ob[k, at(r // 2), at(r // 2)], ob[k, at(2 + r // 2), at(2 + r // 2)]
                qp[k, at(r), at(r)] = jnp.where(z == 0, a, b)
            else:
                qp[k, at(r), at(r)] = jnp.where(ci > ri, db[k, at(r), at(r)], db[k, at(r + 1), at(r + 1)])

    def send_diagonals():
        for k in range(SUB):
            for r in range(4):
                own = jnp.where(ri == ci, db[k, at(r), at(r)].astype(F32), 0.0)
                dg[4 * k + r : 4 * k + r + 1, :] = jnp.sum(own, axis=0, keepdims=True)
        diag[x] = dg[...].astype(BF16)
        start(*diagonals())

    def diagonals():
        return [
            remote(diag.at[x], diag.at[x], d_s.at[i], d_r.at[x], to) for i, to in enumerate((right, left, across))
        ]

    def merge_diagonals():
        for i in (x1, x2, x3):
            arrived(diag.at[i], d_r.at[i])
        t = [diag[i].astype(F32) for i in range(RING)]
        dg[...] = ((t[0] + t[1]) + (t[2] + t[3])).astype(BF16).astype(F32) * 0.5

    def add_to_partial(k):
        arrived(near.at[k, 1], ld.at[k, 2])
        part[k, 0] = (come(k, 0) + near[k, 1].astype(F32)).astype(BF16)
        partial(k)[0].start()
        part[k, 1] = (come(k, 3) + qp[k, quarter(x3), :].astype(F32)).astype(BF16)
        partial(k)[1].start()

    def merge(k):
        arrived(near.at[k, 0], ld.at[k, 3])
        m[k, 0, quarter(x), :] = (come(k, 2) + come(k, 1) + near[k, 0].astype(F32)).astype(BF16)
        gather(k, 0, 0, right).start()
        m[k, 1, quarter(x), :] = (come(k, 5) + come(k, 4) + qp[k, quarter(x), :].astype(F32)).astype(BF16)
        gather(k, 1, 1, left).start()

    def gather(k, t, side, to):
        return remote(
            m.at[k, t, quarter(x)], m.at[k, t, quarter(x)], ag_s.at[k, side, t], ag_r.at[k, side, t], to
        )

    def gather_rest(k):
        return gather(k, 1, 0, right), gather(k, 0, 1, left)

    def relay(k, t):
        rows, to = (quarter(x3), right) if t == 0 else (quarter(x1), left)
        return remote(m.at[k, t, rows], m.at[k, t, rows], ag_s.at[k, t, 2], ag_r.at[k, t, 2], to)

    def start_relay(k):
        arrived(m.at[k, 0, quarter(x3)], ag_r.at[k, 0, 0])
        relay(k, 0).start()
        arrived(m.at[k, 1, quarter(x1)], ag_r.at[k, 1, 1])
        relay(k, 1).start()

    def gathered(k):
        arrived(m.at[k, 1, quarter(x3)], ag_r.at[k, 0, 1])
        arrived(m.at[k, 0, quarter(x1)], ag_r.at[k, 1, 0])
        arrived(m.at[k, 0, quarter(x2)], ag_r.at[k, 0, 2])
        arrived(m.at[k, 1, quarter(x2)], ag_r.at[k, 1, 2])

    def to_other(k):
        return remote(modes.at[0, k], vz.at[k], v_s.at[k, 0], v_r.at[k, 0], other)

    def to_twin(k, src):
        return remote(src, vn.at[k], v_s.at[k, 1], v_r.at[k, 1], twin)

    def pass_modes(k):
        arrived(vz.at[k], v_r.at[k, 0])

        @pl.when(core == 0)
        def _():
            to_twin(k, vz.at[k]).start()

    def project(k):
        gathered(k)
        row = lax.broadcasted_iota(jnp.int32, (N, N), 0) // Q
        column = lax.broadcasted_iota(jnp.int32, (N, N), 1) // Q
        both = m[k, 1]
        zero = jnp.zeros_like(both)
        db[k] = jnp.where(column > row, both, zero)
        ob[k] = jnp.where(column < row, both, zero)
        for r in range(4):
            two = m[k, 1, at(r // 2 * 2), at(r // 2 * 2)].astype(F32)
            half = dg[4 * k + r : 4 * k + r + 1, :]
            beside = ci < ri if r % 2 else ci > ri
            db[k, at(r), at(r)] = jnp.where(ri == ci, half, jnp.where(beside, two, 0.0)).astype(BF16)
            lone = m[k, 1, at(r % 2 * 2 + 1), at(r % 2 * 2 + 1)]
            ob[k, at(r), at(r)] = jnp.where(z == r // 2, lone, jnp.zeros_like(lone))
        arrived(vo.at[k], ld.at[k, 4])
        arrived(vn.at[k], v_r.at[k, 1])
        p = (dot(m[k, 0], vn[k]) + dot(db[k], vo[k]) + dot(ob[k], vz[k])).astype(BF16)
        red[k] = dot_rows(vo[k], p) + dot_rows(p, vo[k])
        start(*swap_cores(k))

    def slab(i, c):
        return pl.ds(pl.multiple_of((2 * i + c) * Q, Q), Q)

    def swap_cores(k):
        return [
            remote(red.at[k, slab(i, 1 - core)], red_c.at[k, i], r_s.at[k, j], r_r.at[k, i], twin)
            for j, i in enumerate((1 - z, z))
        ]

    def swap_chips(k):
        src, dst = (last_s, last_z) if k == SUB - 1 else (red_s.at[k], red_z.at[k])
        return remote(src, dst, r_s.at[k, 2], r_r.at[k, 2], other)

    def add_cores(k):
        arrived(red_c.at[k, 1 - z], r_r.at[k, 1 - z])
        away = red[k, slab(1 - z, core), :] + red_c[k, 1 - z]
        if k == SUB - 1:
            last_s[...] = away.astype(BF16)
        else:
            red_s[k] = away
        swap_chips(k).start()
        arrived(red_c.at[k, z], r_r.at[k, z])
        red_c[k, z] = red[k, slab(z, core), :] + red_c[k, z]

    def finish(k):
        if k == SUB - 1:
            arrived(last_z, r_r.at[k, 2])
            red_c[k, z] = red_c[k, z] + last_z[...].astype(F32)
        else:
            arrived(red_z.at[k], r_r.at[k, 2])
            red_c[k, z] = red_c[k, z] + red_z[k]
        result(k).start()

    def result(k):
        return pltpu.make_async_copy(red_c.at[k, z], out.at[k], o_s.at[k])

    for k in range(SUB):
        load(k)

    barrier = pltpu.get_barrier_semaphore()
    for device in (right, left, across, twin, other):
        pl.semaphore_signal(barrier, inc=1, device_id=device, device_id_type=MESH)
    pl.semaphore_wait(barrier, 5)

    start(*raw(0)[:2])
    to_other(0).start()

    @pl.when(core == 1)
    def _():
        for k in range(SUB):
            to_twin(k, modes.at[0, k]).start()

    pack(0)
    start(*raw(0)[2:])
    start(*raw(1)[:2])
    to_other(1).start()
    pack(1)
    start(*raw(1)[2:])
    to_other(2).start()
    add_to_partial(0)
    start(*raw(2)[:2])
    pack(2)
    start(*raw(2)[2:])
    send_diagonals()
    add_to_partial(1)
    merge(0)
    start(*gather_rest(0))
    pass_modes(0)
    add_to_partial(2)
    start_relay(0)
    merge(1)
    start(*gather_rest(1))
    pass_modes(1)
    merge_diagonals()
    project(0)
    merge(2)
    add_cores(0)
    start_relay(1)
    start(*gather_rest(2))
    pass_modes(2)
    start_relay(2)
    finish(0)
    project(1)
    add_cores(1)
    project(2)
    add_cores(2)
    finish(1)
    finish(2)

    for k in range(SUB):
        copies = [*raw(k), *partial(k), gather(k, 0, 0, right), gather(k, 1, 1, left), *gather_rest(k)]
        copies += [relay(k, 0), relay(k, 1), to_other(k), to_twin(k, vz.at[k]), *swap_cores(k), swap_chips(k)]
        for c in copies:
            c.wait_send()
        result(k).wait()
    for c in diagonals():
        c.wait_send()


def shards(schur, modes, counts):
    dma = pltpu.SemaphoreType.DMA
    pinned = pl.BlockSpec(memory_space=pltpu.HBM)
    reduced = pl.pallas_call(
        kernel,
        out_shape=jax.ShapeDtypeStruct((SUB, Q, N), F32),
        in_specs=[pinned, pinned],
        out_specs=ANY,
        scratch_shapes=[
            pltpu.VMEM((SUB, N, N), BF16),
            pltpu.VMEM((SUB, N, N), BF16),
            pltpu.VMEM((SUB, N, N), BF16),
            pltpu.VMEM((SUB, 2, Q, N), BF16),
            pltpu.VMEM((SUB, 6, Q, N), BF16),
            pltpu.VMEM((SUB, 2, Q, N), BF16),
            pltpu.VMEM((SUB, 2, N, N), BF16),
            pltpu.VMEM((RING, 16, Q), BF16),
            pltpu.VMEM((16, Q), F32),
            pltpu.VMEM((SUB, N, N), BF16),
            pltpu.VMEM((SUB, N, N), BF16),
            pltpu.VMEM((SUB, N, N), BF16),
            pltpu.VMEM((SUB, N, N), F32),
            pltpu.VMEM((SUB, 2, Q, N), F32),
            pltpu.VMEM((SUB - 1, Q, N), F32),
            pltpu.VMEM((SUB - 1, Q, N), F32),
            pltpu.VMEM((Q, N), BF16),
            pltpu.VMEM((Q, N), BF16),
            dma((SUB, 5)),
            dma((SUB, 6)), dma((SUB, 6)),
            dma((3,)), dma((RING,)),
            dma((SUB, 2, 3)), dma((SUB, 2, 3)),
            dma((SUB, 2)), dma((SUB, 2)),
            dma((SUB, 3)), dma((SUB, 3)),
            dma((SUB,)),
        ],
        compiler_params=pltpu.CompilerParams(
            collective_id=0, has_side_effects=True, vmem_limit_bytes=52 << 20
        ),
        cost_estimate=pl.CostEstimate(flops=5 * SUB * 2 * N**3, bytes_accessed=8 << 20, transcendentals=0),
        name="merge_and_project",
    )(schur, modes)
    row = lax.axis_index("blk") * Q + lax.broadcasted_iota(jnp.int32, reduced.shape, 1)
    column = lax.broadcasted_iota(jnp.int32, reduced.shape, 2)
    kept = counts[0][:, None, None]
    return jnp.where((row < kept) & (column < kept), reduced, 0.0)[None]


def solution(mesh):
    placed = (P("leaf", None, "blk", None), P("leaf", None, "blk", None), P("leaf", None))
    return jax.shard_map(
        shards, mesh=mesh, in_specs=placed, out_specs=P("leaf", None, "blk", None), check_vma=False
    )
```

time: 642 us -> 68 us (0.11)
  waiting for transfers between devices: 579 us -> 0 us
  Pallas kernels: 0 us -> 66.8 us
  other arithmetic: 30.4 us -> 1.02 us
  between operations: 13.2 us -> 0.02 us
  matrix products: 13.1 us -> 0 us
    ppermute x2 -> x0, waiting for transfers between devices: 536 us -> none  [swapped(): lax.ppermute(shard, axis, [(i, i ^ 1 << stride) for i in range(lax.axis_s...]
    pallas_call x0 -> x1, Pallas kernels: none -> 66.8 us  [shards(): pl.pallas_call(kernel, out_shape=jax.ShapeDtypeStruct((SUB, Q, N), F32),...]
    reduce_scatter x1 -> x0, waiting for transfers between devices: 41.6 us -> none  [shards(): reduced = lax.psum_scatter(terms, 'blk', scatter_dimension=1, tiled=True)]
    convert_element_type x2 -> x0, other arithmetic: 16.1 us -> none  [the longest x1 11.8 us: shards(): merged = summed.astype(jnp.bfloat16)]
    add x1, other arithmetic: 14.2 us -> 0.01 us  [shards(): lax.axis_index('blk') * Q]
    dot_general x4 -> x0, matrix products: 13.1 us -> none  [the longest x3 10.4 us: add_rows(): jnp.einsum('ksr,krc->ksc', block, piece, preferred_element_type=jnp.float32)]
  transfers between devices with their start and end apart: 6 -> 0, of which waited for: 3 -> 0; matrix products, arithmetic and copies ran while one was open for 3% -> 0% of each run, Pallas kernels for 0% -> 0%
where the time goes in v2:
time: 68 us; the launch traced here: 67.9 us
  Pallas kernels  66.8 us (98%)
  other arithmetic  1.02 us (2%)
    pallas_call x1, Pallas kernels, shards(): pl.pallas_call(kernel, out_shape=jax.ShapeDtypeStruct((SUB, Q, N), F32),...  66.8 us

profile of v2, /device:TPU:1, one launch (start us, length us, event | category | flops | bytes accessed | tf_op | source)
XLA Modules:
  0.0 67.9 jit_solution(4886361854268909430)
XLA Ops:
  0.0 0.0 copy-start
  0.0 66.8 %merge_and_project.1 = f32[3,128,512]{2,1,0:T(8,128)S(1)} custom-call(bf16[1,3,512,2048]{3,2,1,0:T(8,128)(2,1)} %schur.1, bf16[1,3,512,512]{3,2,1,0:T(8,128)(2,1)} %modes.1), custom_call_target="tpu_custom_call" | custom-call | flops 4026531840 | bytes 8388608 | tf_op jit(solution)/shard_map/merge_and_project/pallas_call | solution.py:301
  66.8 0.0 copy-done
  66.9 1.0 %select_bitcast_fusion = f32[1,3,128,512]{3,2,1,0:T(8,128)} fusion(f32[3,128,512]{2,1,0:T(8,128)S(1)} %merge_and_project.1, s32[3]{0:T(128)S(1)} %bitcast.3, s32[128]{0:T(128)S(1)} %iota_add_fusion), kind=kLoop, calls=%fused_computation | loop fusion | flops 786432 | bytes 1573388 | tf_op jit(solution)/shard_map/broadcast_in_dim | solution.py:342
  (1 shorter events, 0.0 us)
Async XLA Ops:
  0.0 66.8 %copy-start = (s32[1,3]{1,0:T(1,128)S(1)}, s32[1,3]{1,0:T(1,128)}, u32[]{:S(2)}) copy-start(s32[1,3]{1,0:T(1,128)} %param.5) | copy-start | bytes 40

commit v3 on v2

v3 whole, which is shorter than its diff:
```python
import jax
import jax.numpy as jnp
from jax import lax
from jax.experimental import pallas as pl
from jax.experimental.pallas import tpu as pltpu
from jax.sharding import PartitionSpec as P

MESH = pl.DeviceIdType.MESH
ANY = pl.BlockSpec(memory_space=pl.ANY)
F32 = jnp.float32
BF16 = jnp.bfloat16

SUB = 3
N = 512
Q = 128
RING = 4


def dot(a, b):
    return jnp.dot(a, b, preferred_element_type=F32)


def dot_rows(a, b):
    return lax.dot_general(a, b, (((0,), (0,)), ((), ())), preferred_element_type=F32)


def kernel(
    schur, modes, out, out_far,
    db, ob, qp, near, inbox, part, m, diag, dg, halves, vo, vt, vz, p, late, keep, away, far, short, short_far,
    ld, rs_s, rs_r, d_s, d_r, ag_s, ag_r, v_s, v_r, p_s, p_r, r_s, r_r, o_s,
):
    leaf = lax.axis_index("leaf")
    blk = lax.axis_index("blk")
    x = lax.rem(leaf, RING)
    base = leaf - x
    z, core = blk // 2, lax.rem(blk, 2)
    x1, x2, x3 = (lax.rem(x + i, RING) for i in (1, 2, 3))
    right, across, left = ((base + i, blk) for i in (x1, x2, x3))
    twin = (leaf, z * 2 + 1 - core)
    other = (leaf, (1 - z) * 2 + core)

    def columns(i):
        return pl.ds(pl.multiple_of(lax.rem(blk + i, 4) * N, N), N)

    def quarter(d):
        return pl.ds(pl.multiple_of(d * Q, Q), Q)

    def remote(src, dst, send, recv, to):
        return pltpu.make_async_remote_copy(
            src_ref=src, dst_ref=dst, send_sem=send, recv_sem=recv, device_id=to, device_id_type=MESH
        )

    def arrived(ref, sem):
        pltpu.make_async_copy(ref, ref, sem).wait()

    def start(*copies):
        for c in copies:
            c.start()

    def load(k):
        for i, (src, dst) in enumerate((
            (schur.at[0, k, :, columns(0)], db.at[k]),
            (schur.at[0, k, :, columns(2)], ob.at[k]),
            (schur.at[0, k, quarter(x1), columns(1)], near.at[k, 1]),
            (schur.at[0, k, quarter(x), columns(1)], near.at[k, 0]),
            (modes.at[0, k], vo.at[k]),
        )):
            pltpu.make_async_copy(src, dst, ld.at[k, i]).start()

    def raw(k):
        return (
            remote(schur.at[0, k, quarter(x2), columns(1)], inbox.at[k, 0], rs_s.at[k, 0], rs_r.at[k, 0], right),
            remote(schur.at[0, k, quarter(x3), columns(1)], inbox.at[k, 1], rs_s.at[k, 1], rs_r.at[k, 1], left),
            remote(qp.at[k, quarter(x2)], inbox.at[k, 3], rs_s.at[k, 3], rs_r.at[k, 3], left),
            remote(qp.at[k, quarter(x1)], inbox.at[k, 4], rs_s.at[k, 4], rs_r.at[k, 4], right),
        )

    def partial(k):
        return (
            remote(part.at[k, 0], inbox.at[k, 2], rs_s.at[k, 2], rs_r.at[k, 2], right),
            remote(part.at[k, 1], inbox.at[k, 5], rs_s.at[k, 5], rs_r.at[k, 5], left),
        )

    def come(k, i):
        arrived(inbox.at[k, i], rs_r.at[k, i])
        return inbox[k, i].astype(F32)

    def places(blocks):
        row = jnp.concatenate([lax.broadcasted_iota(jnp.int32, (Q, N), 0) + d * Q for d in blocks], axis=0)
        return row, lax.broadcasted_iota(jnp.int32, row.shape, 1)

    def pack(k):
        arrived(db.at[k], ld.at[k, 0])
        arrived(ob.at[k], ld.at[k, 1])
        row, column = places(range(4))
        qp[k] = jnp.where(column > row, db[k], ob[k])

    def send_diagonals():
        row = lax.broadcasted_iota(jnp.int32, (Q, Q), 0)
        column = lax.broadcasted_iota(jnp.int32, (Q, Q), 1)
        for k in range(SUB):
            for r in range(4):
                own = db[k, r * Q : (r + 1) * Q, r * Q : (r + 1) * Q].astype(F32)
                dg[4 * k + r : 4 * k + r + 1, :] = jnp.sum(jnp.where(row == column, own, 0.0), axis=0, keepdims=True)
        diag[x] = dg[...].astype(BF16)
        start(*diagonals())

    def diagonals():
        return [
            remote(diag.at[x], diag.at[x], d_s.at[i], d_r.at[x], to) for i, to in enumerate((right, left, across))
        ]

    def merge_diagonals():
        for i in (x1, x2, x3):
            arrived(diag.at[i], d_r.at[i])
        t = [diag[i].astype(F32) for i in range(RING)]
        dg[...] = ((t[0] + t[1]) + (t[2] + t[3])).astype(BF16).astype(F32) * 0.5
        for k in range(SUB):
            for r in range(4):
                halves[k : k + 1, r * Q : (r + 1) * Q] = dg[4 * k + r : 4 * k + r + 1, :]

    def add_to_partial(k, t):
        if t == 0:
            arrived(near.at[k, 1], ld.at[k, 2])
            part[k, 0] = (come(k, 0) + near[k, 1].astype(F32)).astype(BF16)
        else:
            part[k, 1] = (come(k, 3) + qp[k, quarter(x3), :].astype(F32)).astype(BF16)
        partial(k)[t].start()

    def merge(k, t):
        if t == 0:
            arrived(near.at[k, 0], ld.at[k, 3])
            m[k, 0, quarter(x), :] = (come(k, 2) + come(k, 1) + near[k, 0].astype(F32)).astype(BF16)
        else:
            m[k, 1, quarter(x), :] = (come(k, 5) + come(k, 4) + qp[k, quarter(x), :].astype(F32)).astype(BF16)
        gather_first(k)[t].start()

    def gather_first(k):
        return gather(k, 0, 0, right), gather(k, 1, 1, left)

    def gather(k, t, side, to):
        return remote(
            m.at[k, t, quarter(x)], m.at[k, t, quarter(x)], ag_s.at[k, side, t], ag_r.at[k, side, t], to
        )

    def gather_rest(k):
        return gather(k, 1, 0, right), gather(k, 0, 1, left)

    def relay(k, t):
        rows, to = (quarter(x3), right) if t == 0 else (quarter(x1), left)
        return remote(m.at[k, t, rows], m.at[k, t, rows], ag_s.at[k, t, 2], ag_r.at[k, t, 2], to)

    def start_relay(k, t):
        arrived(m.at[k, t, quarter(x1 if t else x3)], ag_r.at[k, t, t])
        relay(k, t).start()

    def gathered_near(k):
        arrived(m.at[k, 1, quarter(x3)], ag_r.at[k, 0, 1])
        arrived(m.at[k, 0, quarter(x1)], ag_r.at[k, 1, 0])

    def gathered_far(k):
        for t in range(2):
            arrived(m.at[k, t, quarter(x2)], ag_r.at[k, t, 2])

    def to_other(k):
        return remote(modes.at[0, k], vz.at[k], v_s.at[k, 0], v_r.at[k, 0], other)

    def to_twin(k):
        return remote(modes.at[0, k], vt.at[k, 0], v_s.at[k, 1], v_r.at[k, 1], twin)

    def on_to_twin(k):
        return remote(vz.at[k], vt.at[k, 1], v_s.at[k, 2], v_r.at[k, 2], twin)

    def pass_modes(k):
        arrived(vz.at[k], v_r.at[k, 0])

        @pl.when(core == 0)
        def _():
            on_to_twin(k).start()

    def modes_here(k):
        arrived(vo.at[k], ld.at[k, 4])
        arrived(vt.at[k, 0], v_r.at[k, 1])

        @pl.when(core == 1)
        def _():
            arrived(vt.at[k, 1], v_r.at[k, 2])

    def upper(k, blocks, both):
        row, column = places(blocks)
        zero = jnp.zeros_like(both)
        half = jnp.broadcast_to(halves[k : k + 1, :], both.shape).astype(BF16)
        own = jnp.where(column > row, both, jnp.where(column == row, half, zero))
        opposite = jnp.where(column < row, both, jnp.where(column == row, both * 0.5, zero))
        return own, opposite

    def project(k, blocks, following, both):
        own, opposite = upper(k, blocks, both)
        return (dot(following, vt[k, core]) + dot(own, vo[k]) + dot(opposite, vz[k])).astype(BF16)

    def project_blocks(k, *blocks):
        following, both = (jnp.concatenate([m[k, t, quarter(d), :] for d in blocks], axis=0) for t in range(2))
        return project(k, blocks, following, both)

    def swap(k):
        return remote(p.at[k, 0], p.at[k, 1], p_s.at[k], p_r.at[k], twin)

    def swap_late():
        return remote(late.at[0], late.at[1], p_s.at[SUB], p_r.at[SUB], twin)

    def project_all(k):
        gathered_near(k)
        gathered_far(k)
        modes_here(k)
        p[k, 0] = project(k, range(4), m[k, 0], m[k, 1])
        swap(k).start()

    def project_mine(k):
        modes_here(k)
        p[k, 0, quarter(x), :] = project_blocks(k, x)
        p[k, 0, quarter(x2), :] = jnp.zeros((Q, N), BF16)

    def project_sides(k):
        gathered_near(k)
        sides = project_blocks(k, x1, x3)
        p[k, 0, quarter(x1), :] = sides[:Q]
        p[k, 0, quarter(x3), :] = sides[Q:]
        swap(k).start()

    def project_far(k):
        gathered_far(k)
        late[0] = project_blocks(k, x2)
        swap_late().start()

    def slab(i):
        return pl.ds(pl.multiple_of((2 * i + core) * Q, Q), Q)

    def reduced(k, i):
        total = dot_rows(vo[k, :, slab(i)], p[k, 0]) + dot_rows(p[k, 0, :, slab(i)], vo[k])
        return total + dot_rows(vt[k, 0, :, slab(i)], p[k, 1]) + dot_rows(p[k, 1, :, slab(i)], vt[k, 0])

    def reduced_late(k, i):
        total = dot_rows(vo[k, quarter(x2), slab(i)], late[0]) + dot_rows(late[0, :, slab(i)], vo[k, quarter(x2), :])
        total += dot_rows(vt[k, 0, quarter(x2), slab(i)], late[1])
        return total + dot_rows(late[1, :, slab(i)], vt[k, 0, quarter(x2), :])

    def swap_chips(k):
        if k == SUB - 1:
            return remote(short.at[1], out_far, r_s.at[k], r_r.at[k], other)
        if k:
            return remote(short.at[0], short_far, r_s.at[k], r_r.at[k], other)
        return remote(away.at[0], far, r_s.at[k], r_r.at[k], other)

    def reduce_away(k):
        arrived(p.at[k, 1], p_r.at[k])
        away[k] = reduced(k, 1 - z)
        if k == 1:
            short[0] = away[k].astype(BF16)
        if k < SUB - 1:
            swap_chips(k).start()

    def reduce_keep(k):
        keep[k] = reduced(k, z)

    def late_away(k):
        arrived(late.at[1], p_r.at[SUB])
        short[1] = (away[k] + reduced_late(k, 1 - z)).astype(BF16)
        swap_chips(k).start()

    def late_keep(k):
        keep[k] = keep[k] + reduced_late(k, z)
        result(k).start()

    def finish(k):
        there = short_far if k else far
        arrived(there, r_r.at[k])
        keep[k] = keep[k] + there[...].astype(F32)
        result(k).start()

    def result(k):
        return pltpu.make_async_copy(keep.at[k], out.at[k], o_s.at[k])

    for k in range(SUB):
        load(k)

    barrier = pltpu.get_barrier_semaphore()
    for device in (right, left, across, twin, other):
        pl.semaphore_signal(barrier, inc=1, device_id=device, device_id_type=MESH)
    pl.semaphore_wait(barrier, 5)

    start(*raw(0)[:2])
    start(to_other(0), to_twin(0))
    start(to_other(1), to_twin(1))
    start(to_other(2), to_twin(2))
    pack(0)
    start(*raw(0)[2:])
    start(*raw(1)[:2])
    pack(1)
    start(*raw(1)[2:])
    add_to_partial(0, 0)
    add_to_partial(0, 1)
    pack(2)
    send_diagonals()
    add_to_partial(1, 0)
    add_to_partial(1, 1)
    merge(0, 0)
    merge(0, 1)
    start(*gather_rest(0))
    start(*raw(2)[:2])
    start(*raw(2)[2:])
    merge(1, 0)
    merge(1, 1)
    start(*gather_rest(1))
    start_relay(0, 0)
    start_relay(0, 1)
    pass_modes(0)
    merge_diagonals()
    add_to_partial(2, 0)
    add_to_partial(2, 1)
    pass_modes(1)
    start_relay(1, 0)
    start_relay(1, 1)
    project_all(0)
    merge(2, 0)
    merge(2, 1)
    start(*gather_rest(2))
    reduce_away(0)
    reduce_keep(0)
    pass_modes(2)
    project_all(1)
    start_relay(2, 0)
    start_relay(2, 1)
    reduce_away(1)
    reduce_keep(1)
    project_mine(2)
    project_sides(2)
    finish(0)
    reduce_away(2)
    reduce_keep(2)
    project_far(2)
    late_away(2)
    late_keep(2)
    finish(1)
    arrived(out_far, r_r.at[SUB - 1])

    for k in range(SUB):
        copies = [*raw(k), *partial(k), *gather_first(k), *gather_rest(k)]
        copies += [relay(k, 0), relay(k, 1), to_other(k), to_twin(k), swap(k), swap_chips(k)]
        for c in copies:
            c.wait_send()
        result(k).wait()
    for c in (*diagonals(), swap_late()):
        c.wait_send()

    @pl.when(core == 0)
    def _():
        for k in range(SUB):
            on_to_twin(k).wait_send()


def shards(schur, modes, counts):
    dma = pltpu.SemaphoreType.DMA
    reduced, far = pl.pallas_call(
        kernel,
        out_shape=(jax.ShapeDtypeStruct((SUB, Q, N), F32), jax.ShapeDtypeStruct((Q, N), BF16)),
        in_specs=[ANY, ANY],
        out_specs=(ANY, ANY),
        scratch_shapes=[
            pltpu.VMEM((SUB, N, N), BF16),
            pltpu.VMEM((SUB, N, N), BF16),
            pltpu.VMEM((SUB, N, N), BF16),
            pltpu.VMEM((SUB, 2, Q, N), BF16),
            pltpu.VMEM((SUB, 6, Q, N), BF16),
            pltpu.VMEM((SUB, 2, Q, N), BF16),
            pltpu.VMEM((SUB, 2, N, N), BF16),
            pltpu.VMEM((RING, 16, Q), BF16),
            pltpu.VMEM((16, Q), F32),
            pltpu.VMEM((8, N), F32),
            pltpu.VMEM((SUB, N, N), BF16),
            pltpu.VMEM((SUB, 2, N, N), BF16),
            pltpu.VMEM((SUB, N, N), BF16),
            pltpu.VMEM((SUB, 2, N, N), BF16),
            pltpu.VMEM((2, Q, N), BF16),
            pltpu.VMEM((SUB, Q, N), F32),
            pltpu.VMEM((SUB, Q, N), F32),
            pltpu.VMEM((Q, N), F32),
            pltpu.VMEM((2, Q, N), BF16),
            pltpu.VMEM((Q, N), BF16),
            dma((SUB, 5)),
            dma((SUB, 6)), dma((SUB, 6)),
            dma((3,)), dma((RING,)),
            dma((SUB, 2, 3)), dma((SUB, 2, 3)),
            dma((SUB, 3)), dma((SUB, 3)),
            dma((SUB + 1,)), dma((SUB + 1,)),
            dma((SUB,)), dma((SUB,)),
            dma((SUB,)),
        ],
        compiler_params=pltpu.CompilerParams(
            collective_id=0, has_side_effects=True, vmem_limit_bytes=52 << 20
        ),
        cost_estimate=pl.CostEstimate(flops=5 * SUB * 2 * N**3, bytes_accessed=8 << 20, transcendentals=0),
        name="merge_and_project",
    )(schur, modes)
    reduced += jnp.pad(far.astype(F32)[None], ((SUB - 1, 0), (0, 0), (0, 0)))
    row = lax.axis_index("blk") * Q + lax.broadcasted_iota(jnp.int32, reduced.shape, 1)
    column = lax.broadcasted_iota(jnp.int32, reduced.shape, 2)
    kept = counts[0][:, None, None]
    return jnp.where((row < kept) & (column < kept), reduced, 0.0)[None]


def solution(mesh):
    placed = (P("leaf", None, "blk", None), P("leaf", None, "blk", None), P("leaf", None))
    return jax.shard_map(
        shards, mesh=mesh, in_specs=placed, out_specs=P("leaf", None, "blk", None), check_vma=False
    )
```

time: 68 us -> 66 us (0.971); the launches traced: 67.9 us -> 65.1 us
  Pallas kernels: 66.8 us -> 64.1 us
    pallas_call x1, Pallas kernels: 66.8 us -> 64.1 us  [shards(): pl.pallas_call(kernel, out_shape=(jax.ShapeDtypeStruct((SUB, Q, N), F32),...]
where the time goes in v3:
time: 66 us; the launch traced here: 65.1 us
  Pallas kernels  64.1 us (97%)
  other arithmetic  1.02 us (2%)
    pallas_call x1, Pallas kernels, shards(): pl.pallas_call(kernel, out_shape=(jax.ShapeDtypeStruct((SUB, Q, N), F32),...  64.1 us

profile of v3, /device:TPU:1, one launch (start us, length us, event | category | flops | bytes accessed | tf_op | source)
XLA Modules:
  0.0 65.1 jit_solution(12801811558467306695)
XLA Ops:
  0.0 0.0 copy-start
  0.0 64.1 %merge_and_project.1 = (f32[3,128,512]{2,1,0:T(8,128)S(1)}, bf16[128,512]{1,0:T(8,128)(2,1)S(1)}) custom-call(bf16[1,3,512,2048]{3,2,1,0:T(8,128)(2,1)} %schur.1, bf16[1,3,512,512]{3,2,1,0:T(8,128)(2,1)} %modes.1), custom_call_target="tpu_custom_call" | custom-call | flops 4026531840 | bytes 8388608 | tf_op jit(solution)/shard_map/merge_and_project/pallas_call | solution.py:363
  64.1 0.0 copy-done
  64.1 1.0 %select_bitcast_fusion = f32[1,3,128,512]{3,2,1,0:T(8,128)} fusion(f32[3,128,512]{2,1,0:T(8,128)S(1)} %get-tuple-element.7, bf16[1,128,512]{2,1,0:T(8,128)(2,1)S(1)} %bitcast.4, s32[3]{0:T(128)S(1)} %bitcast.5, s32[128]{0:T(128)S(1)} %iota_add_fusion), kind=kLoop, calls=%fused_computation | loop fusion | flops 1179648 | bytes 1704460 | tf_op jit(solution)/shard_map/broadcast_in_dim | solution.py:408
  (1 shorter events, 0.0 us)
Async XLA Ops:
  0.0 64.1 %copy-start = (s32[1,3]{1,0:T(1,128)S(1)}, s32[1,3]{1,0:T(1,128)}, u32[]{:S(2)}) copy-start(s32[1,3]{1,0:T(1,128)} %param.5) | copy-start | bytes 40

commit v4 on v3

--- a/solution.py
+++ b/solution.py
@@ -27,7 +27,7 @@
 def kernel(
     schur, modes, out, out_far,
     db, ob, qp, near, inbox, part, m, diag, dg, halves, vo, vt, vz, p, late, keep, away, far, short, short_far,
-    ld, rs_s, rs_r, d_s, d_r, ag_s, ag_r, v_s, v_r, p_s, p_r, r_s, r_r, o_s,
+    load_sem, sent, raw_sem, diag_sem, all_sem, modes_sem, swap_sem, chip_sem, out_sem,
 ):
     leaf = lax.axis_index("leaf")
     blk = lax.axis_index("blk")
@@ -57,41 +57,33 @@
         for c in copies:
             c.start()
 
-    def load(k):
-        for i, (src, dst) in enumerate((
-            (schur.at[0, k, :, columns(0)], db.at[k]),
-            (schur.at[0, k, :, columns(2)], ob.at[k]),
-            (schur.at[0, k, quarter(x1), columns(1)], near.at[k, 1]),
-            (schur.at[0, k, quarter(x), columns(1)], near.at[k, 0]),
-            (modes.at[0, k], vo.at[k]),
-        )):
-            pltpu.make_async_copy(src, dst, ld.at[k, i]).start()
-
-    def raw(k):
-        return (
-            remote(schur.at[0, k, quarter(x2), columns(1)], inbox.at[k, 0], rs_s.at[k, 0], rs_r.at[k, 0], right),
-            remote(schur.at[0, k, quarter(x3), columns(1)], inbox.at[k, 1], rs_s.at[k, 1], rs_r.at[k, 1], left),
-            remote(qp.at[k, quarter(x2)], inbox.at[k, 3], rs_s.at[k, 3], rs_r.at[k, 3], left),
-            remote(qp.at[k, quarter(x1)], inbox.at[k, 4], rs_s.at[k, 4], rs_r.at[k, 4], right),
-        )
-
-    def partial(k):
-        return (
-            remote(part.at[k, 0], inbox.at[k, 2], rs_s.at[k, 2], rs_r.at[k, 2], right),
-            remote(part.at[k, 1], inbox.at[k, 5], rs_s.at[k, 5], rs_r.at[k, 5], left),
-        )
-
-    def come(k, i):
-        arrived(inbox.at[k, i], rs_r.at[k, i])
-        return inbox[k, i].astype(F32)
+    def load():
+        for k in range(SUB):
+            for i, dst in ((0, db), (2, ob)):
+                pltpu.make_async_copy(schur.at[0, k, :, columns(i)], dst.at[k], load_sem.at[k]).start()
+        for i, d in enumerate((x, x1)):
+            pltpu.make_async_copy(schur.at[0, :, quarter(d), columns(1)], near.at[:, i], load_sem.at[SUB]).start()
+        pltpu.make_async_copy(modes.at[0], vo, load_sem.at[SUB + 1]).start()
+
+    def raw(k, t):
+        def send(i, d, sem, to):
+            src = qp.at[k, quarter(d)] if t else schur.at[0, k, quarter(d), columns(1)]
+            return remote(src, inbox.at[k, i], sent.at[0], raw_sem.at[k, sem], to)
+
+        if t:
+            return send(3, x2, 2, left), send(4, x1, 3, right)
+        return send(0, x2, 0, right), send(1, x3, 1, left)
+
+    def partial(k, t):
+        dst = inbox.at[k, 5 if t else 2]
+        return remote(part.at[k, t], dst, sent.at[1], raw_sem.at[k, 3 if t else 1], left if t else right)
 
     def places(blocks):
         row = jnp.concatenate([lax.broadcasted_iota(jnp.int32, (Q, N), 0) + d * Q for d in blocks], axis=0)
         return row, lax.broadcasted_iota(jnp.int32, row.shape, 1)
 
     def pack(k):
-        arrived(db.at[k], ld.at[k, 0])
-        arrived(ob.at[k], ld.at[k, 1])
+        arrived(p.at[k], load_sem.at[k])
         row, column = places(range(4))
         qp[k] = jnp.where(column > row, db[k], ob[k])
 
@@ -106,13 +98,10 @@
         start(*diagonals())
 
     def diagonals():
-        return [
-            remote(diag.at[x], diag.at[x], d_s.at[i], d_r.at[x], to) for i, to in enumerate((right, left, across))
-        ]
+        return [remote(diag.at[x], diag.at[x], sent.at[2], diag_sem, to) for to in (right, left, across)]
 
     def merge_diagonals():
-        for i in (x1, x2, x3):
-            arrived(diag.at[i], d_r.at[i])
+        arrived(diag.at[pl.ds(0, 3)], diag_sem)
         t = [diag[i].astype(F32) for i in range(RING)]
         dg[...] = ((t[0] + t[1]) + (t[2] + t[3])).astype(BF16).astype(F32) * 0.5
         for k in range(SUB):
@@ -120,71 +109,54 @@
                 halves[k : k + 1, r * Q : (r + 1) * Q] = dg[4 * k + r : 4 * k + r + 1, :]
 
     def add_to_partial(k, t):
-        if t == 0:
-            arrived(near.at[k, 1], ld.at[k, 2])
-            part[k, 0] = (come(k, 0) + near[k, 1].astype(F32)).astype(BF16)
-        else:
-            part[k, 1] = (come(k, 3) + qp[k, quarter(x3), :].astype(F32)).astype(BF16)
-        partial(k)[t].start()
+        arrived(inbox.at[k, 3 * t], raw_sem.at[k, 2 * t])
+        own = qp[k, quarter(x3), :] if t else near[k, 1]
+        part[k, t] = (inbox[k, 3 * t].astype(F32) + own.astype(F32)).astype(BF16)
+        partial(k, t).start()
 
     def merge(k, t):
-        if t == 0:
-            arrived(near.at[k, 0], ld.at[k, 3])
-            m[k, 0, quarter(x), :] = (come(k, 2) + come(k, 1) + near[k, 0].astype(F32)).astype(BF16)
-        else:
-            m[k, 1, quarter(x), :] = (come(k, 5) + come(k, 4) + qp[k, quarter(x), :].astype(F32)).astype(BF16)
-        gather_first(k)[t].start()
-
-    def gather_first(k):
-        return gather(k, 0, 0, right), gather(k, 1, 1, left)
-
-    def gather(k, t, side, to):
-        return remote(
-            m.at[k, t, quarter(x)], m.at[k, t, quarter(x)], ag_s.at[k, side, t], ag_r.at[k, side, t], to
-        )
+        two = pl.ds(3 * t + 1, 2)
+        arrived(inbox.at[k, two], raw_sem.at[k, 2 * t + 1])
+        own = qp[k, quarter(x), :] if t else near[k, 0]
+        total = inbox[k, 3 * t + 2].astype(F32) + inbox[k, 3 * t + 1].astype(F32) + own.astype(F32)
+        m[k, t, quarter(x), :] = total.astype(BF16)
+        gather(k, t, t, t).start()
+
+    def gather(k, t, side, sem):
+        ref = m.at[k, t, quarter(x)]
+        return remote(ref, ref, sent.at[0], all_sem.at[k, sem], left if side else right)
 
     def gather_rest(k):
-        return gather(k, 1, 0, right), gather(k, 0, 1, left)
-
-    def relay(k, t):
-        rows, to = (quarter(x3), right) if t == 0 else (quarter(x1), left)
-        return remote(m.at[k, t, rows], m.at[k, t, rows], ag_s.at[k, t, 2], ag_r.at[k, t, 2], to)
+        return gather(k, 1, 0, 2), gather(k, 0, 1, 2)
 
     def start_relay(k, t):
-        arrived(m.at[k, t, quarter(x1 if t else x3)], ag_r.at[k, t, t])
-        relay(k, t).start()
+        ref = m.at[k, t, quarter(x1 if t else x3)]
+        arrived(ref, all_sem.at[k, t])
+        remote(ref, ref, sent.at[1], all_sem.at[k, 3], left if t else right).start()
 
     def gathered_near(k):
-        arrived(m.at[k, 1, quarter(x3)], ag_r.at[k, 0, 1])
-        arrived(m.at[k, 0, quarter(x1)], ag_r.at[k, 1, 0])
+        arrived(inbox.at[k, pl.ds(0, 2)], all_sem.at[k, 2])
 
     def gathered_far(k):
-        for t in range(2):
-            arrived(m.at[k, t, quarter(x2)], ag_r.at[k, t, 2])
+        arrived(inbox.at[k, pl.ds(0, 2)], all_sem.at[k, 3])
 
     def to_other(k):
-        return remote(modes.at[0, k], vz.at[k], v_s.at[k, 0], v_r.at[k, 0], other)
-
-    def to_twin(k):
-        return remote(modes.at[0, k], vt.at[k, 0], v_s.at[k, 1], v_r.at[k, 1], twin)
-
-    def on_to_twin(k):
-        return remote(vz.at[k], vt.at[k, 1], v_s.at[k, 2], v_r.at[k, 2], twin)
+        return remote(modes.at[0, k], vz.at[k], sent.at[3], modes_sem.at[k], other)
+
+    def to_twin():
+        return remote(modes.at[0], vt.at[:, 0], sent.at[3], modes_sem.at[SUB], twin)
 
     def pass_modes(k):
-        arrived(vz.at[k], v_r.at[k, 0])
+        arrived(vz.at[k], modes_sem.at[k])
 
         @pl.when(core == 0)
         def _():
-            on_to_twin(k).start()
+            remote(vz.at[k], vt.at[k, 1], sent.at[4], modes_sem.at[SUB + 1 + k], twin).start()
 
     def modes_here(k):
-        arrived(vo.at[k], ld.at[k, 4])
-        arrived(vt.at[k, 0], v_r.at[k, 1])
-
         @pl.when(core == 1)
         def _():
-            arrived(vt.at[k, 1], v_r.at[k, 2])
+            arrived(vt.at[k, 1], modes_sem.at[SUB + 1 + k])
 
     def upper(k, blocks, both):
         row, column = places(blocks)
@@ -203,10 +175,10 @@
         return project(k, blocks, following, both)
 
     def swap(k):
-        return remote(p.at[k, 0], p.at[k, 1], p_s.at[k], p_r.at[k], twin)
+        return remote(p.at[k, 0], p.at[k, 1], sent.at[5], swap_sem.at[k], twin)
 
     def swap_late():
-        return remote(late.at[0], late.at[1], p_s.at[SUB], p_r.at[SUB], twin)
+        return remote(late.at[0], late.at[1], sent.at[6], swap_sem.at[SUB], twin)
 
     def project_all(k):
         gathered_near(k)
@@ -245,14 +217,11 @@
         return total + dot_rows(late[1, :, slab(i)], vt[k, 0, quarter(x2), :])
 
     def swap_chips(k):
-        if k == SUB - 1:
-            return remote(short.at[1], out_far, r_s.at[k], r_r.at[k], other)
-        if k:
-            return remote(short.at[0], short_far, r_s.at[k], r_r.at[k], other)
-        return remote(away.at[0], far, r_s.at[k], r_r.at[k], other)
+        src, dst = ((away.at[0], far), (short.at[0], short_far), (short.at[1], out_far))[k]
+        return remote(src, dst, sent.at[6], chip_sem.at[k], other)
 
     def reduce_away(k):
-        arrived(p.at[k, 1], p_r.at[k])
+        arrived(p.at[k, 1], swap_sem.at[k])
         away[k] = reduced(k, 1 - z)
         if k == 1:
             short[0] = away[k].astype(BF16)
@@ -263,7 +232,7 @@
         keep[k] = reduced(k, z)
 
     def late_away(k):
-        arrived(late.at[1], p_r.at[SUB])
+        arrived(late.at[1], swap_sem.at[SUB])
         short[1] = (away[k] + reduced_late(k, 1 - z)).astype(BF16)
         swap_chips(k).start()
 
@@ -273,30 +242,28 @@
 
     def finish(k):
         there = short_far if k else far
-        arrived(there, r_r.at[k])
+        arrived(there, chip_sem.at[k])
         keep[k] = keep[k] + there[...].astype(F32)
         result(k).start()
 
     def result(k):
-        return pltpu.make_async_copy(keep.at[k], out.at[k], o_s.at[k])
-
-    for k in range(SUB):
-        load(k)
+        return pltpu.make_async_copy(keep.at[k], out.at[k], out_sem)
+
+    load()
 
     barrier = pltpu.get_barrier_semaphore()
     for device in (right, left, across, twin, other):
         pl.semaphore_signal(barrier, inc=1, device_id=device, device_id_type=MESH)
     pl.semaphore_wait(barrier, 5)
 
-    start(*raw(0)[:2])
-    start(to_other(0), to_twin(0))
-    start(to_other(1), to_twin(1))
-    start(to_other(2), to_twin(2))
+    start(*raw(0, 0))
+    start(to_other(0), to_other(1), to_other(2), to_twin())
     pack(0)
-    start(*raw(0)[2:])
-    start(*raw(1)[:2])
+    start(*raw(0, 1))
+    start(*raw(1, 0))
     pack(1)
-    start(*raw(1)[2:])
+    start(*raw(1, 1))
+    arrived(near, load_sem.at[SUB])
     add_to_partial(0, 0)
     add_to_partial(0, 1)
     pack(2)
@@ -306,8 +273,7 @@
     merge(0, 0)
     merge(0, 1)
     start(*gather_rest(0))
-    start(*raw(2)[:2])
-    start(*raw(2)[2:])
+    start(*raw(2, 0), *raw(2, 1))
     merge(1, 0)
     merge(1, 1)
     start(*gather_rest(1))
@@ -320,6 +286,8 @@
     pass_modes(1)
     start_relay(1, 0)
     start_relay(1, 1)
+    arrived(vo, load_sem.at[SUB + 1])
+    arrived(vt.at[:, 0], modes_sem.at[SUB])
     project_all(0)
     merge(2, 0)
     merge(2, 1)
@@ -336,26 +304,23 @@
     project_sides(2)
     finish(0)
     reduce_away(2)
+    project_far(2)
     reduce_keep(2)
-    project_far(2)
     late_away(2)
     late_keep(2)
     finish(1)
-    arrived(out_far, r_r.at[SUB - 1])
-
-    for k in range(SUB):
-        copies = [*raw(k), *partial(k), *gather_first(k), *gather_rest(k)]
-        copies += [relay(k, 0), relay(k, 1), to_other(k), to_twin(k), swap(k), swap_chips(k)]
-        for c in copies:
-            c.wait_send()
-        result(k).wait()
-    for c in (*diagonals(), swap_late()):
-        c.wait_send()
+
+    for i, ref in enumerate((m, vz, diag.at[pl.ds(0, 3)], m)):
+        arrived(ref, sent.at[i])
 
     @pl.when(core == 0)
     def _():
-        for k in range(SUB):
-            on_to_twin(k).wait_send()
+        arrived(vz, sent.at[4])
+
+    arrived(vz, sent.at[5])
+    arrived(inbox.at[0, pl.ds(0, 5)], sent.at[6])
+    arrived(keep, out_sem)
+    arrived(out_far, chip_sem.at[SUB - 1])
 
 
 def shards(schur, modes, counts):
@@ -386,14 +351,15 @@
             pltpu.VMEM((Q, N), F32),
             pltpu.VMEM((2, Q, N), BF16),
             pltpu.VMEM((Q, N), BF16),
-            dma((SUB, 5)),
-            dma((SUB, 6)), dma((SUB, 6)),
-            dma((3,)), dma((RING,)),
-            dma((SUB, 2, 3)), dma((SUB, 2, 3)),
-            dma((SUB, 3)), dma((SUB, 3)),
-            dma((SUB + 1,)), dma((SUB + 1,)),
-            dma((SUB,)), dma((SUB,)),
+            dma((SUB + 2,)),
+            dma((7,)),
+            dma((SUB, 4)),
+            dma,
+            dma((SUB, 4)),
+            dma((2 * SUB + 1,)),
+            dma((SUB + 1,)),
             dma((SUB,)),
+            dma,
         ],
         compiler_params=pltpu.CompilerParams(
             collective_id=0, has_side_effects=True, vmem_limit_bytes=52 << 20

time: 66 us -> 65.3 us (0.989)
  no operation moved by 1% of the time
where the time goes in v4:
time: 65.3 us; the launch traced here: 65.1 us
  Pallas kernels  64 us (98%)
  other arithmetic  1.02 us (2%)
    pallas_call x1, Pallas kernels, shards(): pl.pallas_call(kernel, out_shape=(jax.ShapeDtypeStruct((SUB, Q, N), F32),...  64 us

profile of v4, /device:TPU:1, one launch (start us, length us, event | category | flops | bytes accessed | tf_op | source)
XLA Modules:
  0.0 65.1 jit_solution(640030459689670206)
XLA Ops:
  0.0 0.0 copy-start
  0.0 64.0 %merge_and_project.1 = (f32[3,128,512]{2,1,0:T(8,128)S(1)}, bf16[128,512]{1,0:T(8,128)(2,1)S(1)}) custom-call(bf16[1,3,512,2048]{3,2,1,0:T(8,128)(2,1)} %schur.1, bf16[1,3,512,512]{3,2,1,0:T(8,128)(2,1)} %modes.1), custom_call_target="tpu_custom_call" | custom-call | flops 4026531840 | bytes 8388608 | tf_op jit(solution)/shard_map/merge_and_project/pallas_call | solution.py:328
  64.0 0.0 copy-done
  64.0 1.0 %select_bitcast_fusion = f32[1,3,128,512]{3,2,1,0:T(8,128)} fusion(f32[3,128,512]{2,1,0:T(8,128)S(1)} %get-tuple-element.7, bf16[1,128,512]{2,1,0:T(8,128)(2,1)S(1)} %bitcast.4, s32[3]{0:T(128)S(1)} %bitcast.5, s32[128]{0:T(128)S(1)} %iota_add_fusion), kind=kLoop, calls=%fused_computation | loop fusion | flops 1179648 | bytes 1704460 | tf_op jit(solution)/shard_map/broadcast_in_dim | solution.py:374
  (1 shorter events, 0.0 us)
Async XLA Ops:
  0.0 64.0 %copy-start = (s32[1,3]{1,0:T(1,128)S(1)}, s32[1,3]{1,0:T(1,128)}, u32[]{:S(2)}) copy-start(s32[1,3]{1,0:T(1,128)} %param.5) | copy-start | bytes 40

commit v5 on v4

--- a/solution.py
+++ b/solution.py
@@ -26,7 +26,7 @@
 
 def kernel(
     schur, modes, out, out_far,
-    db, ob, qp, near, inbox, part, m, diag, dg, halves, vo, vt, vz, p, late, keep, away, far, short, short_far,
+    db, ob, qp, near, inbox, part, m, diag, dg, halves, vo, vt, vz, p, late, keep, away, far, away_last,
     load_sem, sent, raw_sem, diag_sem, all_sem, modes_sem, swap_sem, chip_sem, out_sem,
 ):
     leaf = lax.axis_index("leaf")
@@ -177,8 +177,11 @@
     def swap(k):
         return remote(p.at[k, 0], p.at[k, 1], sent.at[5], swap_sem.at[k], twin)
 
+    def swap_block(k, d):
+        return remote(p.at[k, 0, quarter(d)], p.at[k, 1, quarter(d)], sent.at[5], swap_sem.at[k], twin)
+
     def swap_late():
-        return remote(late.at[0], late.at[1], sent.at[6], swap_sem.at[SUB], twin)
+        return remote(late.at[0], late.at[1], sent.at[5], swap_sem.at[SUB], twin)
 
     def project_all(k):
         gathered_near(k)
@@ -190,14 +193,16 @@
     def project_mine(k):
         modes_here(k)
         p[k, 0, quarter(x), :] = project_blocks(k, x)
-        p[k, 0, quarter(x2), :] = jnp.zeros((Q, N), BF16)
+        swap_block(k, x).start()
+        for i in range(2):
+            p[k, i, quarter(x2), :] = jnp.zeros((Q, N), BF16)
 
     def project_sides(k):
         gathered_near(k)
         sides = project_blocks(k, x1, x3)
         p[k, 0, quarter(x1), :] = sides[:Q]
         p[k, 0, quarter(x3), :] = sides[Q:]
-        swap(k).start()
+        start(swap_block(k, x1), swap_block(k, x3))
 
     def project_far(k):
         gathered_far(k)
@@ -217,14 +222,12 @@
         return total + dot_rows(late[1, :, slab(i)], vt[k, 0, quarter(x2), :])
 
     def swap_chips(k):
-        src, dst = ((away.at[0], far), (short.at[0], short_far), (short.at[1], out_far))[k]
+        src, dst = (away_last, out_far) if k == SUB - 1 else (away.at[k], far.at[k])
         return remote(src, dst, sent.at[6], chip_sem.at[k], other)
 
     def reduce_away(k):
-        arrived(p.at[k, 1], swap_sem.at[k])
+        arrived(inbox.at[0, pl.ds(0, 3)] if k == SUB - 1 else p.at[k, 1], swap_sem.at[k])
         away[k] = reduced(k, 1 - z)
-        if k == 1:
-            short[0] = away[k].astype(BF16)
         if k < SUB - 1:
             swap_chips(k).start()
 
@@ -233,7 +236,7 @@
 
     def late_away(k):
         arrived(late.at[1], swap_sem.at[SUB])
-        short[1] = (away[k] + reduced_late(k, 1 - z)).astype(BF16)
+        away_last[...] = (away[k] + reduced_late(k, 1 - z)).astype(BF16)
         swap_chips(k).start()
 
     def late_keep(k):
@@ -241,9 +244,8 @@
         result(k).start()
 
     def finish(k):
-        there = short_far if k else far
-        arrived(there, chip_sem.at[k])
-        keep[k] = keep[k] + there[...].astype(F32)
+        arrived(far.at[k], chip_sem.at[k])
+        keep[k] = keep[k] + far[k]
         result(k).start()
 
     def result(k):
@@ -348,8 +350,7 @@
             pltpu.VMEM((2, Q, N), BF16),
             pltpu.VMEM((SUB, Q, N), F32),
             pltpu.VMEM((SUB, Q, N), F32),
-            pltpu.VMEM((Q, N), F32),
-            pltpu.VMEM((2, Q, N), BF16),
+            pltpu.VMEM((SUB - 1, Q, N), F32),
             pltpu.VMEM((Q, N), BF16),
             dma((SUB + 2,)),
             dma((7,)),

time: 65.3 us -> 65 us (level)
  no operation moved by 1% of the time
where the time goes in v5:
time: 65 us; the launch traced here: 64.7 us
  Pallas kernels  63.7 us (98%)
  other arithmetic  1.02 us (2%)
    pallas_call x1, Pallas kernels, shards(): pl.pallas_call(kernel, out_shape=(jax.ShapeDtypeStruct((SUB, Q, N), F32),...  63.7 us

profile of v5, /device:TPU:1, one launch (start us, length us, event | category | flops | bytes accessed | tf_op | source)
XLA Modules:
  0.0 64.7 jit_solution(5190554114578119240)
XLA Ops:
  0.0 0.0 copy-start
  0.0 63.7 %merge_and_project.1 = (f32[3,128,512]{2,1,0:T(8,128)S(1)}, bf16[128,512]{1,0:T(8,128)(2,1)S(1)}) custom-call(bf16[1,3,512,2048]{3,2,1,0:T(8,128)(2,1)} %schur.1, bf16[1,3,512,512]{3,2,1,0:T(8,128)(2,1)} %modes.1), custom_call_target="tpu_custom_call" | custom-call | flops 4026531840 | bytes 8388608 | tf_op jit(solution)/shard_map/merge_and_project/pallas_call | solution.py:330
  63.7 0.0 copy-done
  63.7 1.0 %select_bitcast_fusion = f32[1,3,128,512]{3,2,1,0:T(8,128)} fusion(f32[3,128,512]{2,1,0:T(8,128)S(1)} %get-tuple-element.7, bf16[1,128,512]{2,1,0:T(8,128)(2,1)S(1)} %bitcast.4, s32[3]{0:T(128)S(1)} %bitcast.5, s32[128]{0:T(128)S(1)} %iota_add_fusion), kind=kLoop, calls=%fused_computation | loop fusion | flops 1179648 | bytes 1704460 | tf_op jit(solution)/shard_map/broadcast_in_dim | solution.py:375
  (1 shorter events, 0.0 us)
Async XLA Ops:
  0.0 63.7 %copy-start = (s32[1,3]{1,0:T(1,128)S(1)}, s32[1,3]{1,0:T(1,128)}, u32[]{:S(2)}) copy-start(s32[1,3]{1,0:T(1,128)} %param.5) | copy-start | bytes 40

commit v6 on v5

--- a/solution.py
+++ b/solution.py
@@ -217,9 +217,11 @@
         return total + dot_rows(vt[k, 0, :, slab(i)], p[k, 1]) + dot_rows(p[k, 1, :, slab(i)], vt[k, 0])
 
     def reduced_late(k, i):
-        total = dot_rows(vo[k, quarter(x2), slab(i)], late[0]) + dot_rows(late[0, :, slab(i)], vo[k, quarter(x2), :])
-        total += dot_rows(vt[k, 0, quarter(x2), slab(i)], late[1])
-        return total + dot_rows(late[1, :, slab(i)], vt[k, 0, quarter(x2), :])
+        own, there = vo[k, quarter(x2), :], vt[k, 0, quarter(x2), :]
+        mine = (vo[k, quarter(x2), slab(i)], late[0, :, slab(i)])
+        theirs = (vt[k, 0, quarter(x2), slab(i)], late[1, :, slab(i)])
+        rows = jnp.concatenate([*mine, *theirs], axis=0)
+        return dot_rows(rows, jnp.concatenate([late[0], own, late[1], there], axis=0))
 
     def swap_chips(k):
         src, dst = (away_last, out_far) if k == SUB - 1 else (away.at[k], far.at[k])

time: 65 us -> 64.9 us (level)
  no operation moved by 1% of the time
where the time goes in v6:
time: 64.9 us; the launch traced here: 64.7 us
  Pallas kernels  63.7 us (98%)
  other arithmetic  1.02 us (2%)
    pallas_call x1, Pallas kernels, shards(): pl.pallas_call(kernel, out_shape=(jax.ShapeDtypeStruct((SUB, Q, N), F32),...  63.7 us

profile of v6, /device:TPU:1, one launch (start us, length us, event | category | flops | bytes accessed | tf_op | source)
XLA Modules:
  0.0 64.7 jit_solution(9356074650470469411)
XLA Ops:
  0.0 0.0 copy-start
  0.0 63.7 %merge_and_project.1 = (f32[3,128,512]{2,1,0:T(8,128)S(1)}, bf16[128,512]{1,0:T(8,128)(2,1)S(1)}) custom-call(bf16[1,3,512,2048]{3,2,1,0:T(8,128)(2,1)} %schur.1, bf16[1,3,512,512]{3,2,1,0:T(8,128)(2,1)} %modes.1), custom_call_target="tpu_custom_call" | custom-call | flops 4026531840 | bytes 8388608 | tf_op jit(solution)/shard_map/merge_and_project/pallas_call | solution.py:332
  63.7 0.0 copy-done
  63.7 1.0 %select_bitcast_fusion = f32[1,3,128,512]{3,2,1,0:T(8,128)} fusion(f32[3,128,512]{2,1,0:T(8,128)S(1)} %get-tuple-element.7, bf16[1,128,512]{2,1,0:T(8,128)(2,1)S(1)} %bitcast.4, s32[3]{0:T(128)S(1)} %bitcast.5, s32[128]{0:T(128)S(1)} %iota_add_fusion), kind=kLoop, calls=%fused_computation | loop fusion | flops 1179648 | bytes 1704460 | tf_op jit(solution)/shard_map/broadcast_in_dim | solution.py:377
  (1 shorter events, 0.0 us)
Async XLA Ops:
  0.0 63.7 %copy-start = (s32[1,3]{1,0:T(1,128)S(1)}, s32[1,3]{1,0:T(1,128)}, u32[]{:S(2)}) copy-start(s32[1,3]{1,0:T(1,128)} %param.5) | copy-start | bytes 40
